TPU v7x, 32 devices: a whole 2x2x4 slice. The times are simulated.
32 devices in a mesh: video: 2 (over x), frame: 4 (over z), head: 4 (over y, core).
Axes of the slice: x: 2, y: 2, z: 4, core: 2. Of those that a mesh axis runs over, the one named last changes fastest.
Arguments:
- latents: bfloat16 [2048, 2560], P(('video', 'frame', 'head')), parts along dimension 0, may hold values from -24 to 24
- weights: bfloat16 [2560, 3, 2560], P(None, None, 'head'), may hold values from -0.125 to 0.125
- key_slots: int32 [16, 4, 4], P('frame'), may hold values from 0 to 3, as said below
- key_count: int32 [16, 4], P('frame'), may hold values from 0 to 4, as said below
Outputs:
- attended: bfloat16 [2048, 2560], P(('video', 'frame'), 'head'), parts along dimension 0
There are 2 independent parts, one for each index of `video`. A program takes and returns all parts, laid end to end along the dimension named above; an argument that names none is the same for every part. Nothing has to cross between parts.
Inputs may be any that keep to these rules, and one draw needn't show every extreme that they name: key_slots[a, b, :] is a permutation of the local block numbers of a slab. key_count[a, b] is 4 when query block a lies in slab b; otherwise it is at most max(1, 4 // p), where p is the largest power of two not above the distance between a's slab and b.
All inputs are finite; a program needn't handle non-finite values.
Results may differ from a plain program's by a relative error of at most 0.012.
The roundings to bfloat16 on the way count: a program that leaves them out, or rounds other values in their place, can miss the bound.
Values may be sent and summed in bfloat16 or wider, within the bound.
A program may use at most 128 MiB of HBM per device.

v0:
```python
import jax
import jax.numpy as jnp
from jax import lax
from jax.sharding import PartitionSpec as P

HD = 128
masked_score = -1e30


def on_device(latents, weights, key_slots, key_count):
    width_in = weights.shape[0]
    local_width = weights.shape[2]
    w_joined = weights.reshape(width_in, 3 * local_width)
    joined = jnp.dot(
        lax.all_gather(latents, "head", axis=0, tiled=True),
        w_joined,
        preferred_element_type=jnp.float32,
    ).astype(jnp.bfloat16)
    slab_len = joined.shape[0]
    head_count = local_width // HD
    query_heads = joined[:, :local_width].reshape(slab_len, head_count, HD)
    keys_here = joined[:, local_width : 2 * local_width]
    values_here = joined[:, 2 * local_width :]
    score_scale = HD ** (-0.5)
    blocks_here = key_slots.shape[0]
    slab_total = key_slots.shape[1]
    per_slab = key_slots.shape[2]
    block_rows = slab_len // blocks_here
    all_blocks = slab_total * per_slab
    block_ids = jnp.arange(per_slab, dtype=jnp.int32)
    listed = jnp.any(
        (key_slots[:, :, :, None] == block_ids[None, None, None, :])
        & (block_ids[None, None, :, None] < key_count[:, :, None, None]),
        axis=2,
    )
    allowed = listed.reshape(blocks_here, all_blocks).astype(jnp.float32)

    def compute(state, key_part, value_part, visible):
        row_count = key_part.shape[0]
        top_score, denominator, numerator = state
        scores = (
            jnp.einsum(
                "qhd,khd->hqk",
                query_heads,
                key_part.reshape(row_count, head_count, HD),
                preferred_element_type=jnp.float32,
            )
            * score_scale
        )
        scores = jnp.where(visible[None], scores, masked_score)
        new_top = jnp.maximum(top_score, jnp.max(scores, axis=-1))
        rescale = jnp.exp(top_score - new_top)
        shares = jnp.exp(scores - new_top[:, :, None])
        denominator = denominator * rescale + jnp.sum(shares, axis=-1)
        update = jnp.einsum(
            "hqk,khd->qhd",
            shares.astype(jnp.bfloat16),
            value_part.reshape(row_count, head_count, HD),
            preferred_element_type=jnp.float32,
        )
        numerator = numerator * jnp.transpose(rescale)[:, :, None] + update
        return (new_top, denominator, numerator)

    def attend_rows(running, key_part, value_part, first_row):
        row_count = key_part.shape[0]
        row_blocks = (first_row + jnp.arange(row_count, dtype=jnp.int32)) // block_rows
        onehot = (jnp.arange(all_blocks, dtype=jnp.int32)[:, None] == row_blocks[None, :]).astype(
            jnp.float32
        )
        listed_here = jnp.dot(allowed, onehot) > 0.5
        visible = jnp.broadcast_to(
            listed_here[:, None, :], (blocks_here, block_rows, row_count)
        ).reshape(slab_len, row_count)
        return compute(running, key_part, value_part, visible)

    initial = (
        jnp.full((head_count, slab_len), masked_score, jnp.float32),
        jnp.zeros((head_count, slab_len), jnp.float32),
        jnp.zeros((slab_len, head_count, HD), jnp.float32),
    )
    key_part = lax.all_gather(keys_here, "frame", axis=0, tiled=True)
    value_part = lax.all_gather(values_here, "frame", axis=0, tiled=True)
    row_count = key_part.shape[0]
    step_rows = 512

    def one_block(position, state):
        key_block = lax.dynamic_slice_in_dim(key_part, position * step_rows, step_rows, 0)
        value_block = lax.dynamic_slice_in_dim(value_part, position * step_rows, step_rows, 0)
        return attend_rows(state, key_block, value_block, position * step_rows)

    running = lax.fori_loop(0, row_count // step_rows, one_block, initial)
    top_score, denominator, numerator = running
    mixed = numerator / jnp.transpose(denominator)[:, :, None]
    return mixed.reshape(slab_len, local_width).astype(jnp.bfloat16)


def solution(mesh):
    return jax.shard_map(
        on_device,
        mesh=mesh,
        in_specs=(
            P(("video", "frame", "head"), None),
            P(None, None, "head"),
            P("frame", None, None),
            P("frame", None),
        ),
        out_specs=P(("video", "frame"), "head"),
        check_vma=False,
    )
```

profile of v0, /device:TPU:0, one launch (start us, length us, event | category | flops | bytes accessed | tf_op | source)
XLA Modules:
  0.0 130.2 jit_solution(18211134643761131619)
XLA Ops:
  6.5 0.0 all-gather.4.cloned.1.call-start
  6.5 0.7 all-gather.4.cloned.1.call-update
  7.3 0.0 all-gather.6.cloned.1.call-start
  7.3 13.8 %copy.22 = bf16[2560,3,640]{0,2,1:T(8,128)(2,1)} copy(bf16[2560,3,640]{2,0,1:T(8,128)(2,1)} %param.7) | data formatting | bytes 19660800 | tf_op args[1]
  21.1 8.7 %all-gather.4.cloned.1.call-done = bf16[256,2560]{1,0:T(8,128)(2,1)} async-done(((bf16[64,2560]{1,0:T(8,128)(2,1)}), bf16[256,2560]{1,0:T(8,128)(2,1)}) %all-gather.4.cloned.1.call-update) | async-done | bytes 1310736 | tf_op jit(solution)/shard_map/all_gather | solution.py:15
  29.8 7.1 %convolution_convert_fusion = bf16[256,1920]{1,0:T(8,128)(2,1)S(1)} fusion(bf16[256,2560]{1,0:T(8,128)(2,1)} %all-gather.4.cloned.1.call-done, bf16[2560,1920]{0,1:T(8,128)(2,1)} %bitcast.63), kind=kOutput, calls=%fused_computation.35 | convolution fusion | flops 2517073920 | bytes 12124160 | tf_op jit(solution)/shard_map/dot_general | solution.py:14
  36.9 0.0 copy-start.1
  37.0 0.0 copy-start
  37.0 0.9 fusion.26
  37.9 0.0 all-gather.6.cloned.1.call-update
  37.9 0.0 all-gather.8.cloned.1.call-start
  38.0 0.7 all-gather.8.cloned.1.call-update
  38.7 0.0 copy-done.1
  38.7 0.1 iota_compare_fusion.3
  38.8 0.0 copy-done
  38.8 0.1 fusion.25
  38.9 0.1 reshape.69
  39.0 0.2 copy.23
  39.2 0.9 copy.25
  40.1 30.7 %all-gather.6.cloned.1.call-done = bf16[1024,640]{1,0:T(8,128)(2,1)} async-done(((bf16[256,640]{1,0:T(8,128)(2,1)}), bf16[1024,640]{1,0:T(8,128)(2,1)}) %all-gather.6.cloned.1.call-update) | async-done | bytes 1310736 | tf_op jit(solution)/shard_map/all_gather | solution.py:81
  70.8 33.3 %all-gather.8.cloned.1.call-done = bf16[1024,640]{1,0:T(8,128)(2,1)} async-done(((bf16[256,640]{1,0:T(8,128)(2,1)}), bf16[1024,640]{1,0:T(8,128)(2,1)}) %all-gather.8.cloned.1.call-update) | async-done | bytes 1310736 | tf_op jit(solution)/shard_map/all_gather | solution.py:82
  104.1 17.6 %while.20 = (s32[]{:T(128)}, f32[5,256]{1,0:T(8,128)S(1)}, f32[5,256]{1,0:T(8,128)S(1)}, f32[256,5,128]{0,2,1:T(8,128)}, bf16[4,16]{1,0:T(4,128)(2,1)S(1)}, /*in...) while((s32[]{:T(128)}, f32[5,256]{1,0:T(8,128)S(1)}, ...), condition=%wide.region_4.5_spmd.clone, body=%wide.region_1.4_spmd.clone.sunk | while | flops 343336448 | bytes 16933176 | solution.py:91
  104.1 2.2 %constant_dynamic-slice_fusion.3 = (bf16[512,640]{1,0:T(8,128)(2,1)}, bf16[512,640]{1,0:T(8,128)(2,1)S(1)}) fusion(bf16[1024,640]{1,0:T(8,128)(2,1)} %get-tuple-element.375, s32[]{:T(128)S(6)} %select_n.63, bf16[1024,640]{1,0:T(8,128)(2,1)} %get-tuple-element.373), kind=kLoop, calls=%fused_computation.31.clone.1 | loop fusion | bytes 2621444 | tf_op jit(solution)/shard_map/while/body/eval_jaxpr/dynamic_slice | solution.py:88
  106.3 0.2 copy.36
  106.6 0.1 fusion.49
  106.8 0.3 copy.35
  107.0 1.6 %fusion.50 = (f32[5,256]{1,0:T(8,128)S(1)}, f32[5,512,256]{2,1,0:T(8,128)S(1)}) fusion(pred[256,512]{0,1:T(8,128)(4,1)S(1)} %copy.35, bf16[512,5,128]{0,2,1:T(8,128)(2,1)S(1)} %bitcast.60, bf16[256,5,128]{2,0,1:T(8,128)(2,1)} %get-tuple-element.374), kind=kOutput, calls=%fused_computation.4.clone.1 | convolution fusion | flops 169736960 | bytes 3740672 | tf_op jit(solution)/shard_map/while/body/eval_jaxpr/qhd,khd->hqk/dot_general | solution.py:42
  108.7 1.3 %copy.37 = bf16[512,640]{0,1:T(8,128)(2,1)S(1)} copy(bf16[512,640]{1,0:T(8,128)(2,1)} %get-tuple-element.342) | data formatting | bytes 1310720 | tf_op jit(solution)/shard_map/while/body/eval_jaxpr/dynamic_slice | solution.py:88
  110.0 1.7 %fusion.54 = f32[256,5,128]{0,2,1:T(8,128)} fusion(bf16[512,5,128]{0,2,1:T(8,128)(2,1)S(1)} %bitcast.61, f32[5,512,256]{2,1,0:T(8,128)S(1)} %get-tuple-element.341, f32[5,256]{1,0:T(8,128)S(1)} %get-tuple-element.369, pred[256,512]{0,1:T(8,128)(4,1)S(1)} %copy.35, f32[256,5,128]{0,2,1:T(8,128)} %get-tuple-element.359, ...), kind=kOutput, calls=%fused_computation.11.clone.1 | convolution fusion | flops 170885120 | bytes 4728833 | tf_op jit(solution)/shard_map/while/body/eval_jaxpr/hqk,khd->qhd/dot_general | solution.py:55
  111.7 0.6 fusion.52
  112.3 2.2 %constant_dynamic-slice_fusion.3 = (bf16[512,640]{1,0:T(8,128)(2,1)}, bf16[512,640]{1,0:T(8,128)(2,1)S(1)}) fusion(bf16[1024,640]{1,0:T(8,128)(2,1)} %get-tuple-element.375, s32[]{:T(128)S(6)} %select_n.63, bf16[1024,640]{1,0:T(8,128)(2,1)} %get-tuple-element.373), kind=kLoop, calls=%fused_computation.31.clone.1 | loop fusion | bytes 2621444 | tf_op jit(solution)/shard_map/while/body/eval_jaxpr/dynamic_slice | solution.py:88
  114.6 0.2 copy.36
  114.8 0.1 fusion.49
  115.0 0.3 copy.35
  115.3 1.6 %fusion.50 = (f32[5,256]{1,0:T(8,128)S(1)}, f32[5,512,256]{2,1,0:T(8,128)S(1)}) fusion(pred[256,512]{0,1:T(8,128)(4,1)S(1)} %copy.35, bf16[512,5,128]{0,2,1:T(8,128)(2,1)S(1)} %bitcast.60, bf16[256,5,128]{2,0,1:T(8,128)(2,1)} %get-tuple-element.374), kind=kOutput, calls=%fused_computation.4.clone.1 | convolution fusion | flops 169736960 | bytes 3740672 | tf_op jit(solution)/shard_map/while/body/eval_jaxpr/qhd,khd->hqk/dot_general | solution.py:42
  116.9 1.3 %copy.37 = bf16[512,640]{0,1:T(8,128)(2,1)S(1)} copy(bf16[512,640]{1,0:T(8,128)(2,1)} %get-tuple-element.342) | data formatting | bytes 1310720 | tf_op jit(solution)/shard_map/while/body/eval_jaxpr/dynamic_slice | solution.py:88
  118.3 2.8 %fusion.54 = f32[256,5,128]{0,2,1:T(8,128)} fusion(bf16[512,5,128]{0,2,1:T(8,128)(2,1)S(1)} %bitcast.61, f32[5,512,256]{2,1,0:T(8,128)S(1)} %get-tuple-element.341, f32[5,256]{1,0:T(8,128)S(1)} %get-tuple-element.369, pred[256,512]{0,1:T(8,128)(4,1)S(1)} %copy.35, f32[256,5,128]{0,2,1:T(8,128)} %get-tuple-element.359, ...), kind=kOutput, calls=%fused_computation.11.clone.1 | convolution fusion | flops 170885120 | bytes 4728833 | tf_op jit(solution)/shard_map/while/body/eval_jaxpr/hqk,khd->qhd/dot_general | solution.py:55
  121.0 0.6 fusion.52
  121.6 1.1 divide_convert_fusion
  122.8 0.9 copy.27
  (14 shorter events, 0.2 us)
Async XLA Ops:
  6.5 23.3 %all-gather.4.cloned.1.call-start = ((), (), s32[]{:S(2)}) async-start(), calls=%async_computation | async-start | bytes 1638400 | tf_op jit(solution)/shard_map/all_gather | solution.py:15
  7.3 63.5 %all-gather.6.cloned.1.call-start = ((), (), s32[]{:S(2)}) async-start(), calls=%async_computation.1 | async-start | bytes 1638400 | tf_op jit(solution)/shard_map/all_gather | solution.py:81
  36.9 1.7 %copy-start.1 = (s32[4,4]{1,0:T(4,128)S(1)}, s32[4,4]{1,0:T(4,128)}, u32[]{:S(2)}) copy-start(s32[4,4]{1,0:T(4,128)} %param.9) | copy-start | bytes 196
  37.0 1.8 %copy-start = (s32[4,4,4]{2,1,0:T(4,128)S(1)}, s32[4,4,4]{2,1,0:T(4,128)}, u32[]{:S(2)}) copy-start(s32[4,4,4]{2,1,0:T(4,128)} %param.8) | copy-start | bytes 772
  37.9 66.2 %all-gather.8.cloned.1.call-start = ((), (), s32[]{:S(2)}) async-start(), calls=%async_computation.2 | async-start | bytes 1638400 | tf_op jit(solution)/shard_map/all_gather | solution.py:82
Sparse Core Ops, SparseCore 0:
  8.9 20.8 all-gather.3
  38.0 32.6 all-gather.5
  72.3 31.6 all-gather.7
where the time goes:
time: 131 us; the launch traced here: 130 us
  waiting for transfers between devices  74.1 us (57%)
  local copies, waits for them, and re-layouts  25.1 us (19%)
  matrix products  15.1 us (12%)
  between operations  13.2 us (10%)
  other arithmetic  2.52 us (2%)
    all_gather x1, waiting for transfers between devices, on_device(): value_part = lax.all_gather(values_here, 'frame', axis=0, tiled=True)  33.3 us
    all_gather x1, waiting for transfers between devices, on_device(): key_part = lax.all_gather(keys_here, 'frame', axis=0, tiled=True)  30.7 us
    unnamed x6, local copies, waits for them, and re-layouts  14.7 us
    all_gather x1, waiting for transfers between devices, on_device(): lax.all_gather(latents, 'head', axis=0, tiled=True)  8.7 us
    dynamic_slice x4, local copies, waits for them, and re-layouts, one_block(): lax.dynamic_slice_in_dim(value_part, position * step_rows, step_rows, 0)  7.14 us
    dot_general x1, matrix products, on_device(): jnp.dot(lax.all_gather(latents, 'head', axis=0, tiled=True), w_joined, pr...  7.09 us
    dot_general x2, matrix products, compute(): jnp.einsum('hqk,khd->qhd', shares.astype(jnp.bfloat16), value_part.reshap...  4.46 us
    dot_general x2, matrix products, compute(): jnp.einsum('qhd,khd->hqk', query_heads, key_part.reshape(row_count, head_...  3.27 us
  transfers between devices with their start and end apart: 3, of which 3 were waited for; matrix products, arithmetic and copies ran while one was open for 12% of the time, Pallas kernels for 0%

commit v1 on v0

--- a/solution.py
+++ b/solution.py
@@ -5,6 +5,16 @@
 
 HD = 128
 masked_score = -1e30
+
+
+def gather_around(x, axis, dim):
+    ways, here, step = (lax.axis_size(axis), lax.axis_index(axis), x.shape[dim])
+    dims = [n * ways if d == dim else n for d, n in enumerate(x.shape)]
+    full = lax.dynamic_update_slice_in_dim(jnp.zeros(dims, x.dtype), x, here * step, axis=dim)
+    for far in range(1, ways):
+        x = lax.ppermute(x, axis, [(d, (d + 1) % ways) for d in range(ways)])
+        full = lax.dynamic_update_slice_in_dim(full, x, (here - far) % ways * step, axis=dim)
+    return full
 
 
 def on_device(latents, weights, key_slots, key_count):
@@ -79,7 +89,7 @@
         jnp.zeros((slab_len, head_count, HD), jnp.float32),
     )
     key_part = lax.all_gather(keys_here, "frame", axis=0, tiled=True)
-    value_part = lax.all_gather(values_here, "frame", axis=0, tiled=True)
+    value_part = gather_around(values_here, "frame", 0)
     row_count = key_part.shape[0]
     step_rows = 512
 

time: 131 us -> 111 us (0.85)
  waiting for transfers between devices: 74.1 us -> 44.5 us
  starting transfers between devices: 0.08 us -> 6.69 us
  local copies, waits for them, and re-layouts: 25.1 us -> 27.5 us
    ppermute x0 -> x3, waiting for transfers between devices: none -> 35.1 us  [gather_around(): x = lax.ppermute(x, axis, [(d, (d + 1) % ways) for d in range(ways)])]
    all_gather x1 -> x0, waiting for transfers between devices: 33.3 us -> none  [on_device(): value_part = lax.all_gather(values_here, 'frame', axis=0, tiled=True)]
    all_gather x1, waiting for transfers between devices: 30.7 us -> 0.01 us  [on_device(): key_part = lax.all_gather(keys_here, 'frame', axis=0, tiled=True)]
    ppermute x0 -> x3, starting transfers between devices: none -> 6.65 us  [gather_around(): x = lax.ppermute(x, axis, [(d, (d + 1) % ways) for d in range(ways)])]
    dynamic_slice x4 -> x2, local copies, waits for them, and re-layouts: 7.14 us -> 2.28 us  [one_block(): lax.dynamic_slice_in_dim(value_part, position * step_rows, step_rows, 0)]
    dynamic_update_slice x0 -> x4, local copies, waits for them, and re-layouts: none -> 3.18 us  [the longest x3 2.38 us: gather_around(): lax.dynamic_update_slice_in_dim(full, x, (here - far) % ways * step, axis...]
    dynamic_slice x2 -> x4, local copies, waits for them, and re-layouts: 0.5 us -> 2.8 us  [one_block(): lax.dynamic_slice_in_dim(key_part, position * step_rows, step_rows, 0)]
  transfers between devices with their start and end apart: 3 -> 5, of which waited for: 3 -> 4; matrix products, arithmetic and copies ran while one was open for 12% -> 18% of each run, Pallas kernels for 0% -> 0%
where the time goes in v1:
time: 111 us; the launch traced here: 110 us
  waiting for transfers between devices  44.5 us (40%)
  local copies, waits for them, and re-layouts  27.5 us (25%)
  matrix products  15.1 us (14%)
  between operations  13.5 us (12%)
  starting transfers between devices  6.69 us (6%)
  other arithmetic  2.52 us (2%)
    ppermute x3, waiting for transfers between devices, gather_around(): x = lax.ppermute(x, axis, [(d, (d + 1) % ways) for d in range(ways)])  35.1 us
    unnamed x6, local copies, waits for them, and re-layouts  14.8 us
    all_gather x1, waiting for transfers between devices, on_device(): lax.all_gather(latents, 'head', axis=0, tiled=True)  8.69 us
    dot_general x1, matrix products, on_device(): jnp.dot(lax.all_gather(latents, 'head', axis=0, tiled=True), w_joined, pr...  7.12 us
    ppermute x3, starting transfers between devices, gather_around(): x = lax.ppermute(x, axis, [(d, (d + 1) % ways) for d in range(ways)])  6.65 us
    dot_general x2, matrix products, compute(): jnp.einsum('hqk,khd->qhd', shares.astype(jnp.bfloat16), value_part.reshap...  4.47 us
    dot_general x2, matrix products, compute(): jnp.einsum('qhd,khd->hqk', query_heads, key_part.reshape(row_count, head_...  3.26 us
    dynamic_slice x4, local copies, waits for them, and re-layouts, one_block(): lax.dynamic_slice_in_dim(key_part, position * step_rows, step_rows, 0)  2.8 us
  transfers between devices with their start and end apart: 5, of which 4 were waited for; matrix products, arithmetic and copies ran while one was open for 18% of the time, Pallas kernels for 0%

profile of v1, /device:TPU:0, one launch (start us, length us, event | category | flops | bytes accessed | tf_op | source)
XLA Modules:
  0.0 110.0 jit_solution(1039178783722528607)
XLA Ops:
  6.5 0.0 all-gather.3.cloned.1.call-start
  6.5 0.7 all-gather.3.cloned.1.call-update
  7.3 0.0 all-gather.5.cloned.1.call-start
  7.3 13.9 %copy.28 = bf16[2560,3,640]{0,2,1:T(8,128)(2,1)} copy(bf16[2560,3,640]{2,0,1:T(8,128)(2,1)} %param.7) | data formatting | bytes 19660800 | tf_op args[1]
  21.2 8.7 %all-gather.3.cloned.1.call-done = bf16[256,2560]{1,0:T(8,128)(2,1)} async-done(((bf16[64,2560]{1,0:T(8,128)(2,1)}), bf16[256,2560]{1,0:T(8,128)(2,1)}) %all-gather.3.cloned.1.call-update) | async-done | bytes 1310736 | tf_op jit(solution)/shard_map/all_gather | solution.py:25
  29.8 0.0 copy-start.1
  29.8 0.0 copy-start
  29.8 7.1 %convolution_convert_fusion = bf16[256,1920]{1,0:T(8,128)(2,1)S(1)} fusion(bf16[256,2560]{1,0:T(8,128)(2,1)} %all-gather.3.cloned.1.call-done, bf16[2560,1920]{0,1:T(8,128)(2,1)} %bitcast.63), kind=kOutput, calls=%fused_computation.35 | convolution fusion | flops 2517073920 | bytes 12124160 | tf_op jit(solution)/shard_map/dot_general | solution.py:24
  37.0 0.8 fusion.26
  37.8 0.0 all-gather.5.cloned.1.call-update
  37.8 1.5 %collective-permute-start = (bf16[256,640]{1,0:T(8,128)(2,1)S(1)}, bf16[256,640]{1,0:T(8,128)(2,1)S(1)}, u32[]{:S(2)}, u32[]{:S(2)}) collective-permute-start(bf16[256,640]{1,0:T(8,128)(2,1)S(1)} %get-tuple-element.278), channel_id=1, source_target_pairs={{0,4},{4,8},{8,12},{12,0},{1,5},{5,9},{9,13},{13,1},{2,6},{6,10},{... | collective-permute-start | bytes 983048 | tf_op jit(solution)/shard_map/ppermute | solution.py:15
  39.3 10.3 %collective-permute-done = bf16[256,640]{1,0:T(8,128)(2,1)S(1)} collective-permute-done((bf16[256,640]{1,0:T(8,128)(2,1)S(1)}, bf16[256,640]{1,0:T(8,128)(2,1)S(1)}, u32[]{:S(2)}, u32[]{:S(2)}) %collective-permute-start) | collective-permute-done | bytes 327712 | tf_op jit(solution)/shard_map/ppermute | solution.py:15
  49.6 0.8 collective-permute-start.1
  50.4 0.0 copy-done.1
  50.4 0.1 iota_compare_fusion.3
  50.5 0.0 copy-done
  50.5 0.1 fusion.25
  50.6 0.1 reshape.69
  50.7 0.2 copy.30
  50.9 0.2 copy.29
  51.1 0.9 copy.35
  52.0 16.5 %collective-permute-done.1 = bf16[256,640]{1,0:T(8,128)(2,1)S(1)} collective-permute-done((bf16[256,640]{1,0:T(8,128)(2,1)S(1)}, bf16[256,640]{1,0:T(8,128)(2,1)S(1)}, u32[]{:S(2)}, u32[]{:S(2)}) %collective-permute-start.1) | collective-permute-done | bytes 327712 | tf_op jit(solution)/shard_map/ppermute | solution.py:15
  68.4 4.3 %collective-permute-start.2 = (bf16[256,640]{1,0:T(8,128)(2,1)S(1)}, bf16[256,640]{1,0:T(8,128)(2,1)S(1)}, u32[]{:S(2)}, u32[]{:S(2)}) collective-permute-start(bf16[256,640]{1,0:T(8,128)(2,1)S(1)} %collective-permute-done.1), channel_id=1, source_target_pairs={{0,4},{4,8},{8,12},{12,0},{1,5},{5,9},{9,13},{13,1},{2,6},{6,10},{... | collective-permute-start | bytes 983048 | tf_op jit(solution)/shard_map/ppermute | solution.py:15
  72.8 1.2 %broadcast_in_dim.88 = bf16[1024,640]{0,1:T(8,128)(2,1)} broadcast(bf16[]{:T(256)} %constant.161.clone.1), dimensions={} | broadcast | bytes 1310722 | tf_op jit(solution)/shard_map/broadcast_in_dim | solution.py:13
  74.0 0.8 constant_dynamic-update-slice_fusion.3
  74.8 0.2 copy.31
  75.0 0.8 constant_dynamic-update-slice_fusion.2
  75.8 0.2 copy.32
  76.0 0.8 constant_dynamic-update-slice_fusion.1
  76.8 8.4 %collective-permute-done.2 = bf16[256,640]{1,0:T(8,128)(2,1)S(1)} collective-permute-done((bf16[256,640]{1,0:T(8,128)(2,1)S(1)}, bf16[256,640]{1,0:T(8,128)(2,1)S(1)}, u32[]{:S(2)}, u32[]{:S(2)}) %collective-permute-start.2) | collective-permute-done | bytes 327712 | tf_op jit(solution)/shard_map/ppermute | solution.py:15
  85.2 0.2 copy.33
  85.4 0.8 constant_dynamic-update-slice_fusion
  86.1 0.0 all-gather.5.cloned.1.call-done
  86.1 15.0 %while.20 = (s32[]{:T(128)}, f32[5,256]{1,0:T(8,128)S(1)}, f32[5,256]{1,0:T(8,128)S(1)}, f32[256,5,128]{0,2,1:T(8,128)}, bf16[4,16]{1,0:T(4,128)(2,1)S(1)}, /*in...) while((s32[]{:T(128)}, f32[5,256]{1,0:T(8,128)S(1)}, ...), condition=%wide.region_4.5_spmd.clone, body=%wide.region_1.4_spmd.clone.sunk | while | flops 343336448 | bytes 15622459 | solution.py:101
  86.1 1.1 %constant_dynamic-slice_fusion.4 = bf16[512,640]{1,0:T(8,128)(2,1)S(1)} fusion(bf16[1024,640]{1,0:T(8,128)(2,1)} %get-tuple-element.367, s32[]{:T(128)S(6)} %select_n.97), kind=kLoop, calls=%fused_computation.32.clone.1 | loop fusion | bytes 1310724 | tf_op jit(solution)/shard_map/while/body/eval_jaxpr/dynamic_slice | solution.py:97
  87.3 0.3 copy.43
  87.5 0.1 fusion.49
  87.7 0.3 copy.42
  88.0 1.6 %fusion.50 = (f32[5,256]{1,0:T(8,128)S(1)}, f32[5,512,256]{2,1,0:T(8,128)S(1)}) fusion(pred[256,512]{0,1:T(8,128)(4,1)S(1)} %copy.42, bf16[512,5,128]{0,2,1:T(8,128)(2,1)S(1)} %bitcast.60, bf16[256,5,128]{2,0,1:T(8,128)(2,1)} %get-tuple-element.368), kind=kOutput, calls=%fused_computation.4.clone.1 | convolution fusion | flops 169736960 | bytes 3740672 | tf_op jit(solution)/shard_map/while/body/eval_jaxpr/qhd,khd->hqk/dot_general | solution.py:52
  89.7 1.1 %constant_dynamic-slice_fusion.5 = bf16[512,640]{0,1:T(8,128)(2,1)S(1)} fusion(bf16[1024,640]{0,1:T(8,128)(2,1)} %get-tuple-element.369, s32[]{:T(128)S(6)} %select_n.97), kind=kLoop, calls=%fused_computation.31.clone.1 | loop fusion | bytes 1310724 | tf_op jit(solution)/shard_map/while/body/eval_jaxpr/dynamic_slice | solution.py:98
  90.8 1.7 %fusion.54 = f32[256,5,128]{0,2,1:T(8,128)} fusion(bf16[512,5,128]{0,2,1:T(8,128)(2,1)S(1)} %bitcast.61, f32[5,512,256]{2,1,0:T(8,128)S(1)} %get-tuple-element.336, f32[5,256]{1,0:T(8,128)S(1)} %get-tuple-element.363, pred[256,512]{0,1:T(8,128)(4,1)S(1)} %copy.42, f32[256,5,128]{0,2,1:T(8,128)} %get-tuple-element.353, ...), kind=kOutput, calls=%fused_computation.11.clone.1 | convolution fusion | flops 170885120 | bytes 4728833 | tf_op jit(solution)/shard_map/while/body/eval_jaxpr/hqk,khd->qhd/dot_general | solution.py:65
  92.5 0.6 fusion.52
  93.1 1.1 %constant_dynamic-slice_fusion.4 = bf16[512,640]{1,0:T(8,128)(2,1)S(1)} fusion(bf16[1024,640]{1,0:T(8,128)(2,1)} %get-tuple-element.367, s32[]{:T(128)S(6)} %select_n.97), kind=kLoop, calls=%fused_computation.32.clone.1 | loop fusion | bytes 1310724 | tf_op jit(solution)/shard_map/while/body/eval_jaxpr/dynamic_slice | solution.py:97
  94.2 0.3 copy.43
  94.5 0.1 fusion.49
  94.7 0.3 copy.42
  95.0 1.6 %fusion.50 = (f32[5,256]{1,0:T(8,128)S(1)}, f32[5,512,256]{2,1,0:T(8,128)S(1)}) fusion(pred[256,512]{0,1:T(8,128)(4,1)S(1)} %copy.42, bf16[512,5,128]{0,2,1:T(8,128)(2,1)S(1)} %bitcast.60, bf16[256,5,128]{2,0,1:T(8,128)(2,1)} %get-tuple-element.368), kind=kOutput, calls=%fused_computation.4.clone.1 | convolution fusion | flops 169736960 | bytes 3740672 | tf_op jit(solution)/shard_map/while/body/eval_jaxpr/qhd,khd->hqk/dot_general | solution.py:52
  96.6 1.1 %constant_dynamic-slice_fusion.5 = bf16[512,640]{0,1:T(8,128)(2,1)S(1)} fusion(bf16[1024,640]{0,1:T(8,128)(2,1)} %get-tuple-element.369, s32[]{:T(128)S(6)} %select_n.97), kind=kLoop, calls=%fused_computation.31.clone.1 | loop fusion | bytes 1310724 | tf_op jit(solution)/shard_map/while/body/eval_jaxpr/dynamic_slice | solution.py:98
  97.8 2.8 %fusion.54 = f32[256,5,128]{0,2,1:T(8,128)} fusion(bf16[512,5,128]{0,2,1:T(8,128)(2,1)S(1)} %bitcast.61, f32[5,512,256]{2,1,0:T(8,128)S(1)} %get-tuple-element.336, f32[5,256]{1,0:T(8,128)S(1)} %get-tuple-element.363, pred[256,512]{0,1:T(8,128)(4,1)S(1)} %copy.42, f32[256,5,128]{0,2,1:T(8,128)} %get-tuple-element.353, ...), kind=kOutput, calls=%fused_computation.11.clone.1 | convolution fusion | flops 170885120 | bytes 4728833 | tf_op jit(solution)/shard_map/while/body/eval_jaxpr/hqk,khd->qhd/dot_general | solution.py:65
  100.5 0.6 fusion.52
  101.1 1.1 %divide_convert_fusion = bf16[256,5,128]{0,2,1:T(8,128)(2,1)S(1)} fusion(f32[256,5,128]{0,2,1:T(8,128)} %get-tuple-element.205, f32[256,5]{0,1:T(8,128)S(1)} %bitcast.66), kind=kLoop, calls=%fused_computation.36 | loop fusion | flops 327680 | bytes 988160 | tf_op jit(solution)/shard_map/convert_element_type | solution.py:104
  102.3 0.9 copy.36
  (14 shorter events, 0.2 us)
Async XLA Ops:
  6.5 23.3 %all-gather.3.cloned.1.call-start = ((), (), s32[]{:S(2)}) async-start(), calls=%async_computation | async-start | bytes 1638400 | tf_op jit(solution)/shard_map/all_gather | solution.py:25
  7.3 78.9 %all-gather.5.cloned.1.call-start = ((), (), s32[]{:S(2)}) async-start(), calls=%async_computation.1 | async-start | bytes 1638400 | tf_op jit(solution)/shard_map/all_gather | solution.py:91
  29.8 20.6 %copy-start.1 = (s32[4,4]{1,0:T(4,128)S(1)}, s32[4,4]{1,0:T(4,128)}, u32[]{:S(2)}) copy-start(s32[4,4]{1,0:T(4,128)} %param.9) | copy-start | bytes 196
  29.8 20.6 %copy-start = (s32[4,4,4]{2,1,0:T(4,128)S(1)}, s32[4,4,4]{2,1,0:T(4,128)}, u32[]{:S(2)}) copy-start(s32[4,4,4]{2,1,0:T(4,128)} %param.8) | copy-start | bytes 772
  37.8 11.8 %collective-permute-start = (bf16[256,640]{1,0:T(8,128)(2,1)S(1)}, bf16[256,640]{1,0:T(8,128)(2,1)S(1)}, u32[]{:S(2)}, u32[]{:S(2)}) collective-permute-start(bf16[256,640]{1,0:T(8,128)(2,1)S(1)} %get-tuple-element.278), channel_id=1, source_target_pairs={{0,4},{4,8},{8,12},{12,0},{1,5},{5,9},{9,13},{13,1},{2,6},{6,10},{... | collective-permute-start | bytes 983048 | tf_op jit(solution)/shard_map/ppermute | solution.py:15
  49.6 18.8 %collective-permute-start.1 = (bf16[256,640]{1,0:T(8,128)(2,1)S(1)}, bf16[256,640]{1,0:T(8,128)(2,1)S(1)}, u32[]{:S(2)}, u32[]{:S(2)}) collective-permute-start(bf16[256,640]{1,0:T(8,128)(2,1)S(1)} %collective-permute-done), channel_id=1, source_target_pairs={{0,4},{4,8},{8,12},{12,0},{1,5},{5,9},{9,13},{13,1},{2,6},{6,10},{... | collective-permute-start | bytes 983048 | tf_op jit(solution)/shard_map/ppermute | solution.py:15
  68.4 16.7 %collective-permute-start.2 = (bf16[256,640]{1,0:T(8,128)(2,1)S(1)}, bf16[256,640]{1,0:T(8,128)(2,1)S(1)}, u32[]{:S(2)}, u32[]{:S(2)}) collective-permute-start(bf16[256,640]{1,0:T(8,128)(2,1)S(1)} %collective-permute-done.1), channel_id=1, source_target_pairs={{0,4},{4,8},{8,12},{12,0},{1,5},{5,9},{9,13},{13,1},{2,6},{6,10},{... | collective-permute-start | bytes 983048 | tf_op jit(solution)/shard_map/ppermute | solution.py:15
Sparse Core Ops, SparseCore 0:
  8.9 20.8 all-gather.2
  37.9 41.6 all-gather.4
